TPU v7x, 32 devices: a whole 2x2x4 slice. The times are simulated.
32 devices in a mesh: exp: 8 (over y, x, core), attn: 4 (over z).
Axes of the slice: x: 2, y: 2, z: 4, core: 2. Of those that a mesh axis runs over, the one named last changes fastest.
Arguments:
- tokens: bfloat16 [1024, 2048], P('exp', 'attn'), may hold values from -6 to 6
- cotangent: bfloat16 [1024, 2048], P('exp', 'attn'), may hold values from -6 to 6
- expert_ids: int32 [1024, 2], P('exp'), may hold values from 0 to 7, all different within a row; in each aligned block of 128 rows (0 to 127, 128 to 255, ...) at most 48 rows name the same one
- route_weight: bfloat16 [1024, 2], P('exp'), may hold values from 0.099609375 to 1
- gate_weight: bfloat16 [8, 2048, 768], P('exp', 'attn'), may hold values from -0.125 to 0.125
- up_weight: bfloat16 [8, 2048, 768], P('exp', 'attn'), may hold values from -0.125 to 0.125
- down_weight: bfloat16 [8, 768, 2048], P('exp', None, 'attn'), may hold values from -0.21875 to 0.21875
Outputs:
- grad_tokens: bfloat16 [1024, 2048], P('exp', 'attn')
- grad_route: float32 [1024, 2], P('exp')
- grad_gate: float32 [8, 2048, 768], P('exp', 'attn')
- grad_up: float32 [8, 2048, 768], P('exp', 'attn')
- grad_down: float32 [8, 768, 2048], P('exp', None, 'attn')
Inputs may be any that keep to these rules, and one draw needn't show every extreme that they name: `expert_ids`: each row names 2 different experts. Within the 128 tokens of one index of exp (aligned blocks of rows), no expert is named by more than 48 choices, and in every draw some block names some expert exactly 48 times.
All inputs are finite; a program needn't handle non-finite values.
Results may differ from a plain program's by a relative error of at most 0.028.
Values may be sent and summed in bfloat16 or wider, within the bound.
A program may use at most 64 MiB of HBM per device.

v0:
```python
import jax
import jax.numpy as jnp
from jax import lax
from jax.sharding import PartitionSpec as P


def swiglu_grads(summed, hidden):
    gate_part = summed[:, :hidden]
    up_part = summed[:, hidden : 2 * hidden]
    back_part = summed[:, 2 * hidden :]
    sigmoid_gate = jax.nn.sigmoid(gate_part)
    silu_gate = gate_part * sigmoid_gate
    activation = silu_gate * up_part
    grad_g = back_part * up_part * sigmoid_gate * (1.0 + gate_part * (1.0 - sigmoid_gate))
    grad_u = back_part * silu_gate
    return jnp.concatenate([activation, grad_g, grad_u], axis=1).astype(jnp.bfloat16)


def shards(tokens, cotangent, expert_ids, route_weight, gate_weight, up_weight, down_weight):
    tok_rows, width_share = tokens.shape
    per_token = expert_ids.shape[1]
    experts = lax.axis_size("exp")
    capacity = 3 * tok_rows * per_token // (2 * experts)
    hidden = gate_weight.shape[2]
    slot_total = experts * capacity
    routed = expert_ids.reshape(-1)
    one_hot = (routed[:, None] == jnp.arange(experts, dtype=jnp.int32)[None, :]).astype(jnp.int32)
    ranked = jnp.cumsum(one_hot, axis=0) - 1
    slot_pos = jnp.sum(ranked * one_hot, axis=1)
    target = routed * capacity + slot_pos
    feat_send = (
        jnp.zeros((slot_total, width_share), jnp.bfloat16)
        .at[target]
        .set(jnp.repeat(tokens, per_token, axis=0))
    )
    upstream_send = (
        jnp.zeros((slot_total, width_share), jnp.bfloat16)
        .at[target]
        .set(jnp.repeat(cotangent, per_token, axis=0))
    )
    weight_send = jnp.zeros((slot_total,), jnp.bfloat16).at[target].set(route_weight.reshape(-1))
    feat_recv, upstream_recv, weight_recv = (
        lax.all_to_all(
            feat_send.reshape(experts, capacity, width_share),
            "exp",
            split_axis=0,
            concat_axis=0,
            tiled=True,
        ),
        lax.all_to_all(
            upstream_send.reshape(experts, capacity, width_share),
            "exp",
            split_axis=0,
            concat_axis=0,
            tiled=True,
        ),
        lax.all_to_all(
            weight_send.reshape(experts, capacity), "exp", split_axis=0, concat_axis=0, tiled=True
        ),
    )
    feat_rows = feat_recv.reshape(slot_total, width_share)
    upstream_rows = upstream_recv.reshape(slot_total, width_share)
    weight_rows = weight_recv.reshape(slot_total)
    scaled_rows = (
        weight_rows[:, None].astype(jnp.float32) * upstream_rows.astype(jnp.float32)
    ).astype(jnp.bfloat16)
    joint_weight = jnp.concatenate([gate_weight[0], up_weight[0]], axis=1)
    down_share = down_weight[0]
    feat_block = feat_rows
    scaled_block = scaled_rows
    gate_up = jnp.dot(feat_block, joint_weight, preferred_element_type=jnp.float32)
    back_hidden = lax.dot_general(
        scaled_block, down_share, (((1,), (1,)), ((), ())), preferred_element_type=jnp.float32
    )
    summed = lax.psum(
        jnp.concatenate([gate_up, back_hidden], axis=1).astype(jnp.bfloat16), "attn"
    ).astype(jnp.float32)
    act_rows = swiglu_grads(summed, hidden)
    feat_block = feat_rows
    scaled_block = scaled_rows
    activation = act_rows[:, :hidden]
    grad_pair = act_rows[:, hidden:]
    grad_joint = lax.dot_general(
        feat_block, grad_pair, (((0,), (0,)), ((), ())), preferred_element_type=jnp.float32
    )
    grad_down_part = lax.dot_general(
        activation, scaled_block, (((0,), (0,)), ((), ())), preferred_element_type=jnp.float32
    )
    token_block = lax.dot_general(
        grad_pair, joint_weight, (((1,), (1,)), ((), ())), preferred_element_type=jnp.float32
    ).astype(jnp.bfloat16)
    out_block = jnp.dot(activation, down_share, preferred_element_type=jnp.float32)
    score_block = jnp.sum(upstream_rows.astype(jnp.float32) * out_block, axis=1).astype(
        jnp.bfloat16
    )
    totals = (grad_joint, grad_down_part, token_block, score_block)
    grad_joint, grad_down_share, token_rows, score_rows = totals
    token_back, score_back = (
        lax.all_to_all(
            token_rows.reshape(experts, capacity, width_share),
            "exp",
            split_axis=0,
            concat_axis=0,
            tiled=True,
        ),
        lax.all_to_all(
            score_rows.reshape(experts, capacity), "exp", split_axis=0, concat_axis=0, tiled=True
        ),
    )
    token_choice = token_back.reshape(slot_total, width_share)[target]
    grad_tokens = jnp.sum(
        token_choice.reshape(tok_rows, per_token, width_share).astype(jnp.float32), axis=1
    ).astype(jnp.bfloat16)
    score_choice = score_back.reshape(slot_total)[target].reshape(tok_rows, per_token)
    grad_route = lax.psum(score_choice.astype(jnp.float32), "attn")
    grad_gate = grad_joint[:, :hidden][None]
    grad_up = grad_joint[:, hidden:][None]
    return (grad_tokens, grad_route, grad_gate, grad_up, grad_down_share[None])


def solution(mesh):
    in_specs = (
        P("exp", "attn"),
        P("exp", "attn"),
        P("exp", None),
        P("exp", None),
        P("exp", "attn", None),
        P("exp", "attn", None),
        P("exp", None, "attn"),
    )
    out_specs = (
        P("exp", "attn"),
        P("exp", None),
        P("exp", "attn", None),
        P("exp", "attn", None),
        P("exp", None, "attn"),
    )
    return jax.shard_map(shards, mesh=mesh, in_specs=in_specs, out_specs=out_specs, check_vma=False)
```

profile of v0, /device:TPU:0, one launch (start us, length us, event | category | flops | bytes accessed | tf_op | source)
XLA Modules:
  0.0 178.0 jit_solution(9939661107278980352)
XLA Ops:
  11.2 2.2 %scatter_custom_fusion.1 = bf16[384]{0:T(512)(128)(2,1)S(1)} fusion(s32[256]{0:T(256)S(1)} %bitcast.45, bf16[256]{0:T(256)(128)(2,1)S(1)} %reshape.176, bf16[]{:T(256)} %constant.7.clone.1), kind=kCustom, calls=%fused_computation.39 | custom fusion | bytes 770 | tf_op jit(solution)/shard_map/scatter | solution.py:41
  14.0 5.2 %all-to-all-start.1 = ((bf16[8,1,48]{2,1,0:T(2,128)(2,1)}), bf16[8,1,48]{2,1,0:T(2,128)(2,1)S(1)}, u32[]{:S(2)}, u32[]{:S(2)}) async-start(bf16[8,1,48]{2,1,0:T(2,128)(2,1)} %all_to_all.25), calls=%async_computation.1 | async-start | bytes 8192 | tf_op jit(solution)/shard_map/all_to_all | solution.py:57
  19.2 1.0 broadcast_in_dim.26
  20.4 2.2 %scatter_custom_fusion.2 = bf16[384,512]{1,0:T(8,128)(2,1)} fusion(s32[256]{0:T(256)S(1)} %bitcast.46, bf16[256,512]{1,0:T(8,128)(2,1)S(1)} %reshape.184, bf16[]{:T(256)} %constant.7.clone.1), kind=kCustom, calls=%fused_computation.27 | custom fusion | bytes 393218 | tf_op jit(solution)/shard_map/scatter | solution.py:39
  22.6 1.2 all-to-all-done.1
  23.8 3.5 %all-to-all-start.2 = ((bf16[8,48,512]{2,1,0:T(8,128)(2,1)}), bf16[8,48,512]{2,1,0:T(8,128)(2,1)S(1)}, u32[]{:S(2)}, u32[]{:S(2)}) async-start(bf16[8,48,512]{2,1,0:T(8,128)(2,1)} %bitcast.9), calls=%async_computation.2 | async-start | bytes 786432 | tf_op jit(solution)/shard_map/all_to_all | solution.py:50
  27.5 2.2 %scatter_custom_fusion = bf16[384,512]{1,0:T(8,128)(2,1)} fusion(s32[256]{0:T(256)S(1)} %bitcast.47, bf16[256,512]{1,0:T(8,128)(2,1)S(1)} %reshape.168, bf16[]{:T(256)} %constant.7.clone.1), kind=kCustom, calls=%fused_computation.29 | custom fusion | bytes 393218 | tf_op jit(solution)/shard_map/scatter | solution.py:34
  29.8 5.8 %all-to-all-done.2 = bf16[8,48,512]{2,1,0:T(8,128)(2,1)S(1)} async-done(((bf16[8,48,512]{2,1,0:T(8,128)(2,1)}), bf16[8,48,512]{2,1,0:T(8,128)(2,1)S(1)}, u32[]{:S(2)}, u32[]{:S(2)}) %all-to-all-start.2) | async-done | bytes 393248 | tf_op jit(solution)/shard_map/all_to_all | solution.py:50
  35.5 3.6 %all-to-all-start = ((bf16[8,48,512]{2,1,0:T(8,128)(2,1)}), bf16[8,48,512]{2,1,0:T(8,128)(2,1)S(1)}, u32[]{:S(2)}, u32[]{:S(2)}) async-start(bf16[8,48,512]{2,1,0:T(8,128)(2,1)} %bitcast.4), calls=%async_computation | async-start | bytes 786432 | tf_op jit(solution)/shard_map/all_to_all | solution.py:43
  39.8 7.6 %all-to-all-done = bf16[8,48,512]{2,1,0:T(8,128)(2,1)S(1)} async-done(((bf16[8,48,512]{2,1,0:T(8,128)(2,1)}), bf16[8,48,512]{2,1,0:T(8,128)(2,1)S(1)}, u32[]{:S(2)}, u32[]{:S(2)}) %all-to-all-start) | async-done | bytes 393248 | tf_op jit(solution)/shard_map/all_to_all | solution.py:43
  47.4 1.9 %convolution_convert_fusion = bf16[384,1536]{1,0:T(8,128)(2,1)S(1)} fusion(bf16[384,512]{1,0:T(8,128)(2,1)S(1)} %bitcast.41, bf16[512,768]{1,0:T(8,128)(2,1)S(1)} %bitcast.50, bf16[512,768]{1,0:T(8,128)(2,1)} %bitcast.52), kind=kOutput, calls=%fused_computation.5 | convolution fusion | flops 607715328 | bytes 3145728 | tf_op jit(solution)/shard_map/dot_general | solution.py:71
  49.3 1.3 pad_maximum_fusion
  51.7 74.0 %all-reduce.2.cloned.1.call-done = bf16[384,2304]{1,0:T(8,128)(2,1)} async-done(((bf16[384,2304]{1,0:T(8,128)(2,1)}), bf16[384,2304]{1,0:T(8,128)(2,1)}) %all-reduce.2.cloned.1.call-update) | async-done | bytes 1769488 | tf_op jit(solution)/shard_map/psum | solution.py:75
  125.7 1.7 convert_element_type.76
  129.3 3.7 %all-to-all-start.4 = ((bf16[8,1,48]{2,1,0:T(2,128)(2,1)}), bf16[8,1,48]{2,1,0:T(2,128)(2,1)S(1)}, u32[]{:S(2)}, u32[]{:S(2)}) async-start(bf16[8,1,48]{2,1,0:T(2,128)(2,1)} %convert_element_type.91), calls=%async_computation.4 | async-start | bytes 8192 | tf_op jit(solution)/shard_map/all_to_all | solution.py:106
  133.0 2.7 %convolution_bitcast_fusion = f32[1,768,512]{2,1,0:T(8,128)} fusion(bf16[384,768]{1,0:T(8,128)(2,1)S(1)} %get-tuple-element.20, bf16[384,512]{1,0:T(8,128)(2,1)} %fusion.2), kind=kOutput, calls=%fused_computation.10 | convolution fusion | flops 301989888 | bytes 2555904 | tf_op jit(solution)/shard_map/dot_general | solution.py:86
  135.7 2.7 %fusion.5 = f32[512,1536]{1,0:T(8,128)} fusion(bf16[384,512]{1,0:T(8,128)(2,1)S(1)} %bitcast.42, bf16[384,768]{1,0:T(8,128)(2,1)S(1)} %get-tuple-element.22, bf16[384,768]{1,0:T(8,128)(2,1)S(1)} %get-tuple-element.21), kind=kOutput, calls=%fused_computation.26 | convolution fusion | flops 606339072 | bytes 4718592 | tf_op jit(solution)/shard_map/dot_general | solution.py:83
  138.4 1.6 convolution_convert_fusion.2
  140.0 4.2 %all-to-all-start.3 = ((bf16[8,48,512]{2,1,0:T(8,128)(2,1)}), bf16[8,48,512]{2,1,0:T(8,128)(2,1)S(1)}, u32[]{:S(2)}, u32[]{:S(2)}) async-start(bf16[8,48,512]{2,1,0:T(8,128)(2,1)} %bitcast.12), calls=%async_computation.3 | async-start | bytes 786432 | tf_op jit(solution)/shard_map/all_to_all | solution.py:99
  144.2 3.7 %slice_bitcast_fusion = (f32[1,512,768]{2,1,0:T(8,128)}, f32[1,512,768]{2,1,0:T(8,128)}) fusion(f32[512,1536]{1,0:T(8,128)} %fusion.5), kind=kLoop, calls=%fused_computation.7 | loop fusion | bytes 6291456 | tf_op jit(solution)/shard_map/broadcast_in_dim | solution.py:117
  148.0 1.9 %gather_fusion.1 = bf16[256]{0:T(256)(128)(2,1)S(1)} fusion(bf16[384]{0:T(512)(128)(2,1)S(1)} %reshape.143, s32[1024]{0:T(1024)S(1)} %pad_clamp_fusion), kind=kCustom, calls=%fused_computation.1 | custom fusion | bytes 2048 | tf_op jit(solution)/shard_map/gather | solution.py:114
  150.1 17.8 %psum.15 = f32[128,2]{1,0:T(8,128)S(1)} all-reduce(f32[128,2]{1,0:T(8,128)S(1)} %reshape.146), channel_id=1, replica_groups=mesh['exp'=8,'attn'=4] {'attn'}, use_global_device_ids=true, to_apply=%region_9.10 | all-reduce | flops 256 | bytes 2048 | tf_op jit(solution)/shard_map/psum | solution.py:115
  168.6 1.2 gather_fusion
  169.8 1.3 reduce_sum.34
  (48 shorter events, 9.7 us)
Async XLA Ops:
  7.2 32.2 %copy-start = (bf16[1,768,512]{2,1,0:T(8,128)(2,1)S(1)}, bf16[1,768,512]{2,1,0:T(8,128)(2,1)}, u32[]{:S(2)}) copy-start(bf16[1,768,512]{2,1,0:T(8,128)(2,1)} %param.13) | copy-start | bytes 2359300
  7.2 20.1 %copy-start.1 = (bf16[128,512]{1,0:T(8,128)(2,1)S(1)}, bf16[128,512]{1,0:T(8,128)(2,1)}, u32[]{:S(2)}) copy-start(bf16[128,512]{1,0:T(8,128)(2,1)} %param.7) | copy-start | bytes 393220
  14.0 9.8 %all-to-all-start.1 = ((bf16[8,1,48]{2,1,0:T(2,128)(2,1)}), bf16[8,1,48]{2,1,0:T(2,128)(2,1)S(1)}, u32[]{:S(2)}, u32[]{:S(2)}) async-start(bf16[8,1,48]{2,1,0:T(2,128)(2,1)} %all_to_all.25), calls=%async_computation.1 | async-start | bytes 8192 | tf_op jit(solution)/shard_map/all_to_all | solution.py:57
  23.8 11.7 %all-to-all-start.2 = ((bf16[8,48,512]{2,1,0:T(8,128)(2,1)}), bf16[8,48,512]{2,1,0:T(8,128)(2,1)S(1)}, u32[]{:S(2)}, u32[]{:S(2)}) async-start(bf16[8,48,512]{2,1,0:T(8,128)(2,1)} %bitcast.9), calls=%async_computation.2 | async-start | bytes 786432 | tf_op jit(solution)/shard_map/all_to_all | solution.py:50
  35.5 11.9 %copy-start.2 = (bf16[1,512,768]{2,1,0:T(8,128)(2,1)S(1)}, bf16[1,512,768]{2,1,0:T(8,128)(2,1)}, u32[]{:S(2)}) copy-start(bf16[1,512,768]{2,1,0:T(8,128)(2,1)} %param.12) | copy-start | bytes 2359300
  35.5 11.9 %all-to-all-start = ((bf16[8,48,512]{2,1,0:T(8,128)(2,1)}), bf16[8,48,512]{2,1,0:T(8,128)(2,1)S(1)}, u32[]{:S(2)}, u32[]{:S(2)}) async-start(bf16[8,48,512]{2,1,0:T(8,128)(2,1)} %bitcast.4), calls=%async_computation | async-start | bytes 786432 | tf_op jit(solution)/shard_map/all_to_all | solution.py:43
  39.1 86.6 %all-reduce.2.cloned.1.call-start = ((), (), s32[]{:S(2)}) async-start(), calls=%async_computation.5 | async-start | bytes 3538944 | tf_op jit(solution)/shard_map/psum | solution.py:75
  129.3 10.6 %all-to-all-start.4 = ((bf16[8,1,48]{2,1,0:T(2,128)(2,1)}), bf16[8,1,48]{2,1,0:T(2,128)(2,1)S(1)}, u32[]{:S(2)}, u32[]{:S(2)}) async-start(bf16[8,1,48]{2,1,0:T(2,128)(2,1)} %convert_element_type.91), calls=%async_computation.4 | async-start | bytes 8192 | tf_op jit(solution)/shard_map/all_to_all | solution.py:106
  135.7 2.7 %copy-start.3 = (bf16[1,512,768]{2,1,0:T(8,128)(2,1)S(1)}, bf16[1,512,768]{2,1,0:T(8,128)(2,1)}, u32[]{:S(2)}) copy-start(bf16[1,512,768]{2,1,0:T(8,128)(2,1)} %param.12) | copy-start | bytes 2359300
  135.7 2.7 %copy-start.4 = (bf16[1,512,768]{2,1,0:T(8,128)(2,1)S(1)}, bf16[1,512,768]{2,1,0:T(8,128)(2,1)}, u32[]{:S(2)}) copy-start(bf16[1,512,768]{2,1,0:T(8,128)(2,1)} %param.11) | copy-start | bytes 2359300
  140.0 28.6 %all-to-all-start.3 = ((bf16[8,48,512]{2,1,0:T(8,128)(2,1)}), bf16[8,48,512]{2,1,0:T(8,128)(2,1)S(1)}, u32[]{:S(2)}, u32[]{:S(2)}) async-start(bf16[8,48,512]{2,1,0:T(8,128)(2,1)} %bitcast.12), calls=%async_computation.3 | async-start | bytes 786432 | tf_op jit(solution)/shard_map/all_to_all | solution.py:99
Sparse Core Ops, SparseCore 0:
  50.8 74.8 all-reduce.1
where the time goes:
time: 179 us; the launch traced here: 178 us
  waiting for transfers between devices  88.6 us (49%)
  starting transfers between devices  20.1 us (11%)
  local copies, waits for them, and re-layouts  19.8 us (11%)
  blocking collectives  17.8 us (10%)
  between operations  14.2 us (8%)
  matrix products  9.93 us (6%)
  other arithmetic  7.62 us (4%)
    psum x1, waiting for transfers between devices, shards(): lax.psum(jnp.concatenate([gate_up, back_hidden], axis=1).astype(jnp.bfloa...  74 us
    psum x1, blocking collectives, shards(): grad_route = lax.psum(score_choice.astype(jnp.float32), 'attn')  17.8 us
    all_to_all x1, waiting for transfers between devices, shards(): lax.all_to_all(feat_send.reshape(experts, capacity, width_share), 'exp',...  7.55 us
    all_to_all x1, waiting for transfers between devices, shards(): lax.all_to_all(upstream_send.reshape(experts, capacity, width_share), 'ex...  5.76 us
    all_to_all x1, starting transfers between devices, shards(): lax.all_to_all(weight_send.reshape(experts, capacity), 'exp', split_axis=...  5.17 us
    all_to_all x1, starting transfers between devices, shards(): lax.all_to_all(token_rows.reshape(experts, capacity, width_share), 'exp',...  4.2 us
    broadcast_in_dim x1, local copies, waits for them, and re-layouts, shards(): grad_up = grad_joint[:, hidden:][None]  3.74 us
    all_to_all x1, starting transfers between devices, shards(): lax.all_to_all(score_rows.reshape(experts, capacity), 'exp', split_axis=0...  3.66 us
  transfers between devices with their start and end apart: 6, of which 4 were waited for; matrix products, arithmetic and copies ran while one was open for 12% of the time, Pallas kernels for 0%

commit v1 on v0

--- a/solution.py
+++ b/solution.py
@@ -1,7 +1,368 @@
+import functools
+
 import jax
 import jax.numpy as jnp
 from jax import lax
+from jax.experimental import pallas as pl
+from jax.experimental.pallas import tpu as pltpu
 from jax.sharding import PartitionSpec as P
+
+MESH = pl.DeviceIdType.MESH
+F32 = jnp.float32
+BF16 = jnp.bfloat16
+LAG = 3
+
+
+def partner_of(me, step, count):
+    total, bit = 0, 1
+    while bit < count:
+        total = total + lax.rem(lax.div(me, bit) + lax.div(step, bit), 2) * bit
+        bit *= 2
+    return total
+
+
+def contract_rows(left, right):
+    return lax.dot_general(left, right, (((0,), (0,)), ((), ())), preferred_element_type=F32)
+
+
+def contract_columns(left, right):
+    return lax.dot_general(left, right, (((1,), (1,)), ((), ())), preferred_element_type=F32)
+
+
+def block_kernel(
+    experts, attn, cap,
+    tok_ref, cot_ref, ids_ref, wt_ref, gate_ref, up_ref, down_ref,
+    gtok_ref, route_ref, ggate_ref, gup_ref, gdown_ref,
+    x_send, z_send, x_all, z_all, own, from_left, from_right, to_left, to_right, sums,
+    act_all, gg_all, gu_all, term_send, term_back, acc_gate, acc_up, acc_down,
+    place, score_send, score_back,
+    x_ss, x_rs, z_ss, z_rs, r_ss, r_rs, l_ss, l_rs, t_ss, t_rs, s_ss, s_rs, out_sem,
+):
+    me = lax.axis_index("exp")
+    za = lax.axis_index("attn")
+    tok_rows, width = tok_ref.shape
+    hidden = gate_ref.shape[1]
+    slots = experts * cap
+    last = attn - 1
+
+    def device(step):
+        return (partner_of(me, step, experts), za)
+
+    def block(index):
+        return pl.ds(pl.multiple_of(index * cap, cap), cap)
+
+    barrier = pltpu.get_barrier_semaphore()
+    for step in range(1, experts):
+        pl.semaphore_signal(barrier, inc=1, device_id=device(step), device_id_type=MESH)
+    for step in range(1, attn):
+        pl.semaphore_signal(
+            barrier, inc=1, device_id=(me, lax.rem(za + step, attn)), device_id_type=MESH
+        )
+
+    def x_copy(step):
+        dst = partner_of(me, step, experts)
+        return pltpu.make_async_remote_copy(
+            x_send.at[block(dst)], x_all.at[block(step)], x_ss.at[step], x_rs.at[step],
+            device_id=(dst, za), device_id_type=MESH,
+        )
+
+    def z_copy(step):
+        dst = partner_of(me, step, experts)
+        return pltpu.make_async_remote_copy(
+            z_send.at[block(dst)], z_all.at[block(step)], z_ss.at[step], z_rs.at[step],
+            device_id=(dst, za), device_id_type=MESH,
+        )
+
+    def right_copy(src, piece):
+        return pltpu.make_async_remote_copy(
+            src.at[piece], from_left.at[piece], r_ss.at[piece], r_rs.at[piece],
+            device_id=(me, lax.rem(za + 1, attn)), device_id_type=MESH,
+        )
+
+    def left_copy(src, piece):
+        return pltpu.make_async_remote_copy(
+            src.at[piece], from_right.at[piece], l_ss.at[piece], l_rs.at[piece],
+            device_id=(me, lax.rem(za + attn - 1, attn)), device_id_type=MESH,
+        )
+
+    def term_copy(step):
+        return pltpu.make_async_remote_copy(
+            term_send.at[block(step)], term_back.at[block(me)], t_ss.at[step], t_rs.at[step],
+            device_id=device(step), device_id_type=MESH,
+        )
+
+    def score_copy(step):
+        return pltpu.make_async_remote_copy(
+            score_send, score_back.at[za], s_ss.at[step], s_rs.at[step],
+            device_id=(me, lax.rem(za + step, attn)), device_id_type=MESH,
+        )
+
+    ids = ids_ref[...]
+    lanes = lax.broadcasted_iota(jnp.int32, (tok_rows, slots), 1)
+    first, second = ids[:, 0:1], ids[:, 1:2]
+    named = (lanes[:, :128] == first).astype(F32), (lanes[:, :128] == second).astype(F32)
+    rows = lax.broadcasted_iota(jnp.int32, (tok_rows, tok_rows), 0)
+    cols = lax.broadcasted_iota(jnp.int32, (tok_rows, tok_rows), 1)
+    earlier = (cols < rows).astype(BF16)
+    count = jnp.dot(earlier, (named[0] + named[1]).astype(BF16), preferred_element_type=F32)
+    for j, expert in enumerate((first, second)):
+        rank = jnp.sum(count * named[j], axis=1, keepdims=True).astype(jnp.int32)
+        place[j] = (lanes == expert * cap + rank).astype(F32).astype(BF16)
+    place_0, place_1 = place[0], place[1]
+    weight = wt_ref[...].astype(F32)
+    upstream = cot_ref[...].astype(F32)
+    x_send[...] = contract_rows(place_0 + place_1, tok_ref[...]).astype(BF16)
+    pl.semaphore_wait(barrier, experts - 1 + attn - 1)
+    for step in range(1, experts):
+        x_copy(step).start()
+    z_send[...] = (
+        contract_rows(place_0, (weight[:, 0:1] * upstream).astype(BF16))
+        + contract_rows(place_1, (weight[:, 1:2] * upstream).astype(BF16))
+    ).astype(BF16)
+    for step in range(1, experts):
+        z_copy(step).start()
+    x_all[block(0)] = x_send[block(me)]
+    z_all[block(0)] = z_send[block(me)]
+    share = hidden // attn
+    lane = lax.broadcasted_iota(jnp.int32, (1, hidden), 1)
+    mine = jnp.logical_and(lane >= za * share, lane < (za + 1) * share).astype(F32)
+
+    def send_out(piece):
+        @pl.when(za == 0)
+        def _():
+            right_copy(own, piece).start()
+
+        @pl.when(za == last)
+        def _():
+            left_copy(own, piece).start()
+
+    def pass_right(piece):
+        right_copy(own, piece).wait_recv()
+        to_right[piece] = (from_left[piece].astype(F32) + own[piece].astype(F32)).astype(BF16)
+        right_copy(to_right, piece).start()
+
+    def pass_left(piece):
+        left_copy(own, piece).wait_recv()
+        to_left[piece] = (from_right[piece].astype(F32) + own[piece].astype(F32)).astype(BF16)
+        left_copy(to_left, piece).start()
+
+    middle = jnp.logical_and(za > 0, za < last)
+    low = 2 * za < attn
+
+    def forward(chunk):
+        @pl.when(chunk > 0)
+        def _():
+            x_copy(chunk).wait_recv()
+            z_copy(chunk).wait_recv()
+
+        feat, scaled = x_all[block(chunk)], z_all[block(chunk)]
+        own[3 * chunk] = jnp.dot(feat, gate_ref[...], preferred_element_type=F32).astype(BF16)
+        send_out(3 * chunk)
+        own[3 * chunk + 1] = jnp.dot(feat, up_ref[...], preferred_element_type=F32).astype(BF16)
+        send_out(3 * chunk + 1)
+        own[3 * chunk + 2] = contract_columns(scaled, down_ref[...]).astype(BF16)
+        send_out(3 * chunk + 2)
+
+    def relay(chunk, near):
+        for part in range(3):
+            piece = 3 * chunk + part
+
+            @pl.when(jnp.logical_and(middle, low if near else jnp.logical_not(low)))
+            def _():
+                pass_right(piece)
+
+            @pl.when(jnp.logical_and(middle, jnp.logical_not(low) if near else low))
+            def _():
+                pass_left(piece)
+
+    def finish(chunk):
+        for part in range(3):
+            piece = 3 * chunk + part
+            sums[part] = own[piece].astype(F32)
+
+            @pl.when(za > 0)
+            def _():
+                @pl.when(za == last)
+                def _():
+                    right_copy(own, piece).wait_recv()
+
+                sums[part] = sums[part] + from_left[piece].astype(F32)
+
+            @pl.when(za < last)
+            def _():
+                @pl.when(za == 0)
+                def _():
+                    left_copy(own, piece).wait_recv()
+
+                sums[part] = sums[part] + from_right[piece].astype(F32)
+
+        gate, up, back = sums[0], sums[1], sums[2]
+        sig = 1.0 / (1.0 + jnp.exp(-gate))
+        silu = gate * sig
+        act = (silu * up).astype(BF16)
+        grad_g = (back * up * sig * (1.0 + gate * (1.0 - sig))).astype(BF16)
+        grad_u = (back * silu).astype(BF16)
+        act_all[block(chunk)] = act
+        gg_all[block(chunk)] = grad_g
+        gu_all[block(chunk)] = grad_u
+        term = contract_columns(grad_g, gate_ref[...]) + contract_columns(grad_u, up_ref[...])
+        score = jnp.sum(act.astype(F32) * back * mine, axis=1, keepdims=True)
+        term_send[block(chunk), :width] = term.astype(BF16)
+        term_send[block(chunk), width:] = jnp.broadcast_to(score, (cap, 128)).astype(BF16)
+
+        @pl.when(chunk > 0)
+        def _():
+            term_copy(chunk).start()
+
+        @pl.when(chunk == 0)
+        def _():
+            term_back[block(me)] = term_send[block(0)]
+
+    half = experts // 2 * cap
+
+    def add_grad(acc, left, right, part):
+        lhs = left[pl.ds(part * half, half)]
+        step = 256 if right.shape[1] % 256 == 0 else 128
+        for at in range(0, right.shape[1], step):
+            done = contract_rows(lhs, right[pl.ds(part * half, half), at : at + step])
+            if part:
+                done = acc[:, at : at + step] + done
+            acc[:, at : at + step] = done
+
+    def body(step, carry):
+        @pl.when(step < experts)
+        def _():
+            forward(step)
+
+        @pl.when(jnp.logical_and(step >= 1, step < experts + 1))
+        def _():
+            relay(step - 1, True)
+
+        @pl.when(jnp.logical_and(step >= 2, step < experts + 2))
+        def _():
+            relay(step - 2, False)
+
+        @pl.when(step >= LAG)
+        def _():
+            finish(step - LAG)
+
+        @pl.when(step == LAG + experts // 2 - 1)
+        def _():
+            add_grad(acc_gate, x_all, gg_all, 0)
+            add_grad(acc_up, x_all, gu_all, 0)
+            add_grad(acc_down, act_all, z_all, 0)
+
+        return carry
+
+    lax.fori_loop(0, experts + LAG, body, 0)
+
+    add_grad(acc_gate, x_all, gg_all, 1)
+    gate_out = pltpu.make_async_copy(acc_gate, ggate_ref, out_sem.at[0])
+    gate_out.start()
+    add_grad(acc_up, x_all, gu_all, 1)
+    up_out = pltpu.make_async_copy(acc_up, gup_ref, out_sem.at[1])
+    up_out.start()
+
+    for step in range(1, experts):
+        term_copy(step).wait_recv()
+    place_0, place_1 = place[0], place[1]
+    scores = term_back[:, width:]
+    score_0 = jnp.dot(place_0, scores, preferred_element_type=F32)
+    score_1 = jnp.dot(place_1, scores, preferred_element_type=F32)
+    lane = lax.broadcasted_iota(jnp.int32, (tok_rows, 128), 1)
+    score_send[...] = jnp.transpose(jnp.where(lane == 0, score_0, score_1))[:8]
+    for step in range(1, attn):
+        score_copy(step).start()
+    score_back[za] = score_send[...]
+    gtok_ref[...] = jnp.dot(
+        place_0 + place_1, term_back[:, :width], preferred_element_type=F32
+    ).astype(BF16)
+    add_grad(acc_down, act_all, z_all, 1)
+    down_out = pltpu.make_async_copy(acc_down, gdown_ref, out_sem.at[2])
+    down_out.start()
+    for step in range(1, attn):
+        score_copy(step).wait_recv()
+    total = score_back[0]
+    for index in range(1, attn):
+        total = total + score_back[index]
+    route_ref[...] = jnp.transpose(total)[:, :2] / wt_ref[...].astype(F32)
+
+    for step in range(1, experts):
+        x_copy(step).wait_send()
+        z_copy(step).wait_send()
+        term_copy(step).wait_send()
+    for step in range(1, attn):
+        score_copy(step).wait_send()
+
+    def drain(piece, carry):
+        @pl.when(za < last)
+        def _():
+            right_copy(own, piece).wait_send()
+
+        @pl.when(za > 0)
+        def _():
+            left_copy(own, piece).wait_send()
+
+        return carry
+
+    lax.fori_loop(0, 3 * experts, drain, 0)
+    gate_out.wait()
+    up_out.wait()
+    down_out.wait()
+
+
+def fused_shards(experts, attn, tokens, cotangent, expert_ids, route_weight, gate_weight, up_weight, down_weight):
+    tok_rows, width = tokens.shape
+    per_token = expert_ids.shape[1]
+    cap = 3 * tok_rows * per_token // (2 * experts)
+    hidden = gate_weight.shape[2]
+    slots = experts * cap
+    dma = pltpu.SemaphoreType.DMA
+    vmem = pl.BlockSpec(memory_space=pltpu.VMEM)
+    anywhere = pl.BlockSpec(memory_space=pl.ANY)
+    pieces = pltpu.VMEM((3 * experts, cap, hidden), BF16)
+    grads = pl.pallas_call(
+        functools.partial(block_kernel, experts, attn, cap),
+        out_shape=(
+            jax.ShapeDtypeStruct((tok_rows, width), BF16),
+            jax.ShapeDtypeStruct((tok_rows, per_token), F32),
+            jax.ShapeDtypeStruct((width, hidden), F32),
+            jax.ShapeDtypeStruct((width, hidden), F32),
+            jax.ShapeDtypeStruct((hidden, width), F32),
+        ),
+        in_specs=[vmem] * 7,
+        out_specs=(vmem, vmem, anywhere, anywhere, anywhere),
+        scratch_shapes=[
+            pltpu.VMEM((slots, width), BF16),
+            pltpu.VMEM((slots, width), BF16),
+            pltpu.VMEM((slots, width), BF16),
+            pltpu.VMEM((slots, width), BF16),
+            pieces, pieces, pieces, pieces, pieces,
+            pltpu.VMEM((3, cap, hidden), F32),
+            pltpu.VMEM((slots, hidden), BF16),
+            pltpu.VMEM((slots, hidden), BF16),
+            pltpu.VMEM((slots, hidden), BF16),
+            pltpu.VMEM((slots, width + 128), BF16),
+            pltpu.VMEM((slots, width + 128), BF16),
+            pltpu.VMEM((width, hidden), F32),
+            pltpu.VMEM((width, hidden), F32),
+            pltpu.VMEM((hidden, width), F32),
+            pltpu.VMEM((per_token, tok_rows, slots), BF16),
+            pltpu.VMEM((8, tok_rows), F32),
+            pltpu.VMEM((attn, 8, tok_rows), F32),
+            dma((experts,)), dma((experts,)), dma((experts,)), dma((experts,)),
+            dma((3 * experts,)), dma((3 * experts,)), dma((3 * experts,)), dma((3 * experts,)),
+            dma((experts,)), dma((experts,)),
+            dma((attn,)), dma((attn,)), dma((3,)),
+        ],
+        compiler_params=pltpu.CompilerParams(
+            collective_id=0, has_side_effects=True, vmem_limit_bytes=48 * 1024 * 1024
+        ),
+        cost_estimate=pl.CostEstimate(
+            flops=16 * slots * width * hidden, bytes_accessed=18 * width * hidden, transcendentals=slots * hidden
+        ),
+    )(tokens, cotangent, expert_ids, route_weight, gate_weight[0], up_weight[0], down_weight[0])
+    return (grads[0], grads[1], grads[2][None], grads[3][None], grads[4][None])
 
 
 def swiglu_grads(summed, hidden):
@@ -118,7 +479,25 @@
     return (grad_tokens, grad_route, grad_gate, grad_up, grad_down_share[None])
 
 
+def fits(experts, attn, tokens, expert_ids, hidden):
+    rows, width = tokens.shape[0] // experts, tokens.shape[1] // attn
+    cap = 3 * rows * expert_ids.shape[1] // (2 * experts)
+    return (
+        experts & (experts - 1) == 0
+        and 2 <= experts <= 128
+        and attn >= 2
+        and expert_ids.shape[1] == 2
+        and rows == 128
+        and cap % 16 == 0
+        and width % 128 == 0
+        and hidden % (128 * attn) % 128 == 0
+        and hidden % attn == 0
+    )
+
+
 def solution(mesh):
+    experts, attn = mesh.shape["exp"], mesh.shape["attn"]
+
     in_specs = (
         P("exp", "attn"),
         P("exp", "attn"),
@@ -135,4 +514,14 @@
         P("exp", "attn", None),
         P("exp", None, "attn"),
     )
-    return jax.shard_map(shards, mesh=mesh, in_specs=in_specs, out_specs=out_specs, check_vma=False)
+
+    def whole(tokens, cotangent, expert_ids, route_weight, gate_weight, up_weight, down_weight):
+        args = (tokens, cotangent, expert_ids, route_weight, gate_weight, up_weight, down_weight)
+        part = shards
+        if fits(experts, attn, tokens, expert_ids, gate_weight.shape[2]):
+            part = functools.partial(fused_shards, experts, attn)
+        return jax.shard_map(
+            part, mesh=mesh, in_specs=in_specs, out_specs=out_specs, check_vma=False
+        )(*args)
+
+    return whole

time: 179 us -> 77.9 us (0.44)
  waiting for transfers between devices: 88.6 us -> 0 us
  Pallas kernels: 0 us -> 64.6 us
  starting transfers between devices: 20.1 us -> 0 us
  blocking collectives: 17.8 us -> 0 us
  between operations: 14.2 us -> 0.65 us
  matrix products: 9.93 us -> 0 us
  other arithmetic: 7.62 us -> 0 us
  local copies, waits for them, and re-layouts: 19.8 us -> 12.3 us
    psum x1 -> x0, waiting for transfers between devices: 74 us -> none  [shards(): lax.psum(jnp.concatenate([gate_up, back_hidden], axis=1).astype(jnp.bfloa...]
    pallas_call x0 -> x1, Pallas kernels: none -> 64.6 us  [fused_shards(): pl.pallas_call(functools.partial(block_kernel, experts, attn, cap), out_s...]
    all_to_all x5 -> x0, starting transfers between devices: 20.1 us -> none  [the longest x1 5.17 us: shards(): lax.all_to_all(weight_send.reshape(experts, capacity), 'exp', split_axis=...]
    psum x1 -> x0, blocking collectives: 17.8 us -> none  [shards(): grad_route = lax.psum(score_choice.astype(jnp.float32), 'attn')]
    all_to_all x5 -> x0, waiting for transfers between devices: 14.5 us -> none  [the longest x1 7.55 us: shards(): lax.all_to_all(feat_send.reshape(experts, capacity, width_share), 'exp',...]
    unnamed x13 -> x19, local copies, waits for them, and re-layouts: 2.24 us -> 12.3 us
    dot_general x6 -> x0, matrix products: 9.93 us -> none  [the longest x1 2.74 us: shards(): lax.dot_general(activation, scaled_block, (((0,), (0,)), ((), ())), prefe...]
    scatter x3 -> x0, local copies, waits for them, and re-layouts: 6.64 us -> none  [the longest x1 2.24 us: shards(): upstream_send = jnp.zeros((slot_total, width_share), jnp.bfloat16).at[tar...]
  transfers between devices with their start and end apart: 6 -> 0, of which waited for: 4 -> 0; matrix products, arithmetic and copies ran while one was open for 12% -> 0% of each run, Pallas kernels for 0% -> 0%
where the time goes in v1:
time: 77.9 us; the launch traced here: 77.5 us
  Pallas kernels  64.6 us (83%)
  local copies, waits for them, and re-layouts  12.3 us (16%)
    pallas_call x1, Pallas kernels, fused_shards(): pl.pallas_call(functools.partial(block_kernel, experts, attn, cap), out_s...  64.6 us
    unnamed x19, local copies, waits for them, and re-layouts  12.3 us

profile of v1, /device:TPU:0, one launch (start us, length us, event | category | flops | bytes accessed | tf_op | source)
XLA Modules:
  0.0 77.5 jit_solution(10690317660286972606)
XLA Ops:
  0.6 0.8 %copy.13.wt_ref = bf16[128,2]{1,0:T(8,128)(2,1)S(1)} copy(bf16[128,2]{0,1:T(2,128)(2,1)} %param.10) | data formatting | bytes 1024 | tf_op args[3]
  1.4 0.8 %copy.12.ids_ref = s32[128,2]{1,0:T(8,128)S(1)} copy(s32[128,2]{0,1:T(2,128)} %param.9) | data formatting | bytes 2048 | tf_op args[2]
  2.2 0.0 copy-start
  2.2 1.1 %copy-done = bf16[1,512,768]{2,1,0:T(8,128)(2,1)S(1)} copy-done((bf16[1,512,768]{2,1,0:T(8,128)(2,1)S(1)}, bf16[1,512,768]{2,1,0:T(8,128)(2,1)}, u32[]{:S(2)}) %copy-start) | copy-done | bytes 786456
  3.3 0.0 copy-start.1
  3.3 1.1 %copy-done.1 = bf16[1,512,768]{2,1,0:T(8,128)(2,1)S(1)} copy-done((bf16[1,512,768]{2,1,0:T(8,128)(2,1)S(1)}, bf16[1,512,768]{2,1,0:T(8,128)(2,1)}, u32[]{:S(2)}) %copy-start.1) | copy-done | bytes 786456
  4.5 0.0 copy-start.2
  4.5 1.1 %copy-done.2 = bf16[1,768,512]{2,1,0:T(8,128)(2,1)S(1)} copy-done((bf16[1,768,512]{2,1,0:T(8,128)(2,1)S(1)}, bf16[1,768,512]{2,1,0:T(8,128)(2,1)}, u32[]{:S(2)}) %copy-start.2) | copy-done | bytes 786456
  5.6 0.0 copy-start.3
  5.6 0.9 %copy-done.3 = bf16[128,512]{1,0:T(8,128)(2,1)S(1)} copy-done((bf16[128,512]{1,0:T(8,128)(2,1)S(1)}, bf16[128,512]{1,0:T(8,128)(2,1)}, u32[]{:S(2)}) %copy-start.3) | copy-done | bytes 131096
  6.5 0.0 copy-start.4
  6.5 0.9 %copy-done.4 = bf16[128,512]{1,0:T(8,128)(2,1)S(1)} copy-done((bf16[128,512]{1,0:T(8,128)(2,1)S(1)}, bf16[128,512]{1,0:T(8,128)(2,1)}, u32[]{:S(2)}) %copy-start.4) | copy-done | bytes 131096
  7.4 64.6 %shard_map.110 = (bf16[128,512]{1,0:T(8,128)(2,1)S(1)}, f32[128,2]{1,0:T(8,128)S(1)}, f32[512,768]{1,0:T(8,128)S(1)}, f32[512,768]{1,0:T(8,128)S(1)}, f32[768,512]{1,0:T(8,128)}) custom-call(bf16[128,512]{1,0:T(8,128)(2,1)S(1)} %copy-done.3, bf16[128,512]{1,0:T(8,128)(2,1)S(1)} %copy-done.4, s32[128,2]{1,0:T(8,128)S(1)} %copy.12.ids_ref, ...), custom_call_target="tpu_custom_call" | custom-call | flops 2415919104 | bytes 7077888 | tf_op jit(solution)/shard_map/pallas_call | solution.py:324
  72.0 0.6 copy.14
  72.6 0.7 copy.19
  73.3 1.1 %copy.20 = f32[1,512,768]{2,1,0:T(8,128)} copy(f32[1,512,768]{2,1,0:T(8,128)S(1)} %bitcast.7) | data formatting | bytes 3145728
  74.4 0.0 copy-start.5
  74.4 1.1 %copy.21 = f32[1,512,768]{2,1,0:T(8,128)} copy(f32[1,512,768]{2,1,0:T(8,128)S(1)} %bitcast.6) | data formatting | bytes 3145728
  75.6 0.8 %copy-done.5 = f32[768,512]{1,0:T(8,128)S(1)} copy-done((f32[768,512]{1,0:T(8,128)S(1)}, f32[768,512]{1,0:T(8,128)}, u32[]{:S(2)}) %copy-start.5) | copy-done | bytes 1572888
  76.4 1.1 %copy.22 = f32[1,768,512]{2,1,0:T(8,128)} copy(f32[1,768,512]{2,1,0:T(8,128)S(1)} %bitcast.11) | data formatting | bytes 3145728
Async XLA Ops:
  2.2 1.1 %copy-start = (bf16[1,512,768]{2,1,0:T(8,128)(2,1)S(1)}, bf16[1,512,768]{2,1,0:T(8,128)(2,1)}, u32[]{:S(2)}) copy-start(bf16[1,512,768]{2,1,0:T(8,128)(2,1)} %param.11) | copy-start | bytes 2359300
  3.3 1.1 %copy-start.1 = (bf16[1,512,768]{2,1,0:T(8,128)(2,1)S(1)}, bf16[1,512,768]{2,1,0:T(8,128)(2,1)}, u32[]{:S(2)}) copy-start(bf16[1,512,768]{2,1,0:T(8,128)(2,1)} %param.12) | copy-start | bytes 2359300
  4.5 1.1 %copy-start.2 = (bf16[1,768,512]{2,1,0:T(8,128)(2,1)S(1)}, bf16[1,768,512]{2,1,0:T(8,128)(2,1)}, u32[]{:S(2)}) copy-start(bf16[1,768,512]{2,1,0:T(8,128)(2,1)} %param.13) | copy-start | bytes 2359300
  5.6 0.9 %copy-start.3 = (bf16[128,512]{1,0:T(8,128)(2,1)S(1)}, bf16[128,512]{1,0:T(8,128)(2,1)}, u32[]{:S(2)}) copy-start(bf16[128,512]{1,0:T(8,128)(2,1)} %tok_ref.1) | copy-start | bytes 393220
  6.5 0.9 %copy-start.4 = (bf16[128,512]{1,0:T(8,128)(2,1)S(1)}, bf16[128,512]{1,0:T(8,128)(2,1)}, u32[]{:S(2)}) copy-start(bf16[128,512]{1,0:T(8,128)(2,1)} %cot_ref.1) | copy-start | bytes 393220
  74.4 2.0 %copy-start.5 = (f32[768,512]{1,0:T(8,128)S(1)}, f32[768,512]{1,0:T(8,128)}, u32[]{:S(2)}) copy-start(f32[768,512]{1,0:T(8,128)} %get-tuple-element.14) | copy-start | bytes 4718596
